TPU v7x, 32 devices: a whole 2x2x4 slice. The times are simulated.
32 devices in a mesh: grp: 4 (over y, x), rep: 4 (over z), tp: 2 (over core).
Axes of the slice: x: 2, y: 2, z: 4, core: 2. Of those that a mesh axis runs over, the one named last changes fastest.
Arguments:
- noise_in: bfloat16 [512, 3072], P('rep', 'tp'), may hold values from -6 to 6
- noise_renoise: bfloat16 [512, 3072], P('rep', 'tp'), may hold values from -6 to 6
- text_cond: bfloat16 [4, 3072], P('rep'), may hold values from -3 to 3
- t_index: int32 [4], P('rep'), may hold values from 0 to 999
- gains: float32 [3, 3072], replicated, may hold values from 0.5 to 1.5
- up_weights: bfloat16 [3, 3072, 12288], P(None, 'rep', 'tp'), may hold values from -0.109375 to 0.109375
- down_weights: bfloat16 [3, 12288, 3072], P(None, 'tp', 'rep'), may hold values from -0.0546875 to 0.0546875
Outputs:
- generated: bfloat16 [512, 3072], P('rep', 'tp')
- up_grads: float32 [4, 3072, 12288], P('grp', 'rep', 'tp')
- down_grads: float32 [4, 12288, 3072], P('grp', 'tp', 'rep')
All inputs are finite; a program needn't handle non-finite values. Where the computation divides by a largest or mean magnitude, that divisor is 1e-20 or more.
Results may differ from a plain program's by a relative error of at most 0.01.
Values may be sent and summed in bfloat16 or wider, within the bound.
No kernel may reach another device: no remote copies, remote signals or barrier semaphores. Data moves between devices by JAX's collectives and lax.ppermute only.
A program may use at most 256 MiB of HBM per device.

v0:
```python
import math

import jax
import jax.numpy as jnp
from jax import lax
from jax.sharding import PartitionSpec as P

IMG_TOK = 128


def gelu_tanh(value):
    return jax.nn.gelu(value, approximate=True)


def normalize(whole_rows, own_gain, cond_part):
    values = whole_rows.astype(jnp.float32)
    factor = lax.rsqrt(jnp.mean(values * values, axis=-1, keepdims=True) + 1e-06)
    return (values * factor * own_gain[None, :] * (1.0 + cond_part)).astype(jnp.bfloat16)


def front_pass(inputs, own_gain, cond_part, up_full, down_full, active):
    whole_rows = lax.all_gather(inputs, "tp", axis=1, tiled=True)
    normed = normalize(whole_rows, own_gain, cond_part)
    row_count = normed.shape[0]

    def front_compute():
        hidden_pre = jnp.dot(normed, up_full, preferred_element_type=jnp.float32)
        hidden = gelu_tanh(hidden_pre).astype(jnp.bfloat16)
        return (hidden_pre, hidden, jnp.dot(hidden, down_full, preferred_element_type=jnp.float32))

    def front_skipped():
        return (
            jnp.zeros((row_count, up_full.shape[1]), jnp.float32),
            jnp.zeros((row_count, up_full.shape[1]), jnp.bfloat16),
            jnp.zeros((row_count, down_full.shape[1]), jnp.float32),
        )

    hidden_pre, hidden, partial_terms = lax.cond(active, front_compute, front_skipped)
    summed = lax.psum_scatter(partial_terms, "tp", scatter_dimension=1, tiled=True)
    return (normed, hidden_pre, hidden, summed)


def pre_gradient(upstream, hidden_pre, down_full, active):

    def pre_compute():
        hidden_grad = jnp.dot(upstream, down_full.T, preferred_element_type=jnp.float32)
        return jax.vjp(gelu_tanh, hidden_pre)[1](hidden_grad)[0].astype(jnp.bfloat16)

    def pre_skipped():
        return jnp.zeros(hidden_pre.shape, jnp.bfloat16)

    return lax.cond(active, pre_compute, pre_skipped)


def in_order(half_index, mine_part, other_part):
    first_part = jnp.where(half_index == 0, mine_part, other_part)
    second_part = jnp.where(half_index == 0, other_part, mine_part)
    return jnp.concatenate([first_part, second_part], axis=0)


def padded(half_index, mine_part):
    return in_order(half_index, mine_part, jnp.zeros_like(mine_part))


def body(noise_in, noise_renoise, text_cond, t_index, gains, up_weights, down_weights):
    group_index = lax.axis_index("grp")
    model_index = jnp.maximum(group_index - 1, 0)
    half_index = group_index % 2
    is_student = group_index < 2
    is_teacher = group_index == 2
    is_fake = group_index == 3
    own_up = lax.dynamic_index_in_dim(up_weights, model_index, 0, keepdims=False)
    own_down = lax.dynamic_index_in_dim(down_weights, model_index, 0, keepdims=False)
    up_full, down_full = (
        lax.all_gather(own_up, "rep", axis=0, tiled=True),
        lax.all_gather(own_down, "rep", axis=1, tiled=True),
    )
    own_gain = lax.dynamic_index_in_dim(gains, model_index, 0, keepdims=False)
    cond_rows = jnp.repeat(text_cond.astype(jnp.float32), IMG_TOK, axis=0)
    row_count = noise_in.shape[0]
    half_rows = row_count // 2
    row_start = half_index * half_rows
    student_in = lax.dynamic_slice_in_dim(noise_in, row_start, half_rows, 0)
    cond_half = lax.dynamic_slice_in_dim(cond_rows, row_start, half_rows, 0)
    normed_s, pre_s, hidden_s, summed_s = front_pass(
        student_in, own_gain, cond_half, up_full, down_full, is_student
    )
    own_half = (student_in.astype(jnp.float32) + summed_s).astype(jnp.bfloat16)
    all_groups = lax.all_gather(own_half, "grp", axis=0, tiled=True)
    generated = all_groups[: 2 * half_rows]
    sigma = 0.1 + 0.8 * t_index.astype(jnp.float32) / 999.0
    sigma_rows = jnp.repeat(sigma, IMG_TOK)[:, None]
    noised = (
        (1.0 - sigma_rows) * generated.astype(jnp.float32)
        + sigma_rows * noise_renoise.astype(jnp.float32)
    ).astype(jnp.bfloat16)
    normed_c, pre_c, hidden_c, summed_c = front_pass(
        noised, own_gain, cond_rows, up_full, down_full, jnp.logical_not(is_student)
    )
    predicted = (noised.astype(jnp.float32) + summed_c).astype(jnp.bfloat16).astype(jnp.float32)
    nothing = jnp.zeros_like(predicted)
    real_f, fake_f = lax.psum(
        (jnp.where(is_teacher, predicted, nothing), jnp.where(is_fake, predicted, nothing)), "grp"
    )
    gen_f = generated.astype(jnp.float32)
    images = t_index.shape[0]
    distances = jnp.sum(jnp.abs(gen_f - real_f).reshape(images, IMG_TOK, -1), axis=(1, 2))
    distances = lax.psum(distances, "tp")
    width_all = gen_f.shape[1] * lax.axis_size("tp")
    image_norm = distances / (IMG_TOK * width_all) + 1e-05
    tokens_all = row_count * lax.axis_size("rep")
    push_scale = 1.0 / math.sqrt(tokens_all)
    student_push = (
        (fake_f - real_f) / jnp.repeat(image_norm, IMG_TOK)[:, None] * push_scale
    ).astype(jnp.bfloat16)
    fake_push = ((fake_f - gen_f) * push_scale).astype(jnp.bfloat16)
    push_half = lax.dynamic_slice_in_dim(student_push, row_start, half_rows, 0)
    upstream_s = lax.all_gather(push_half, "tp", axis=1, tiled=True)
    pre_grad_s = pre_gradient(upstream_s, pre_s, down_full, is_student)
    upstream_c = lax.all_gather(fake_push, "tp", axis=1, tiled=True)
    pre_grad_c = pre_gradient(upstream_c, pre_c, down_full, is_fake)
    normed = jnp.where(is_student, padded(half_index, normed_s), normed_c)
    upstream = jnp.where(is_student, padded(half_index, upstream_s), upstream_c)
    hidden = jnp.where(is_student, padded(half_index, hidden_s), hidden_c)
    pre_grad = jnp.where(is_student, padded(half_index, pre_grad_s), pre_grad_c)
    normed_cols, upstream_cols = (
        lax.all_to_all(normed, "rep", split_axis=1, concat_axis=0, tiled=True),
        lax.all_to_all(upstream, "rep", split_axis=1, concat_axis=0, tiled=True),
    )
    hidden_all, pre_grad_all = (
        lax.all_gather(hidden, "rep", axis=0, tiled=True),
        lax.all_gather(pre_grad, "rep", axis=0, tiled=True),
    )

    def weight_grads():
        up_grad = jnp.dot(normed_cols.T, pre_grad_all, preferred_element_type=jnp.float32)
        down_grad = jnp.dot(hidden_all.T, upstream_cols, preferred_element_type=jnp.float32)
        return (up_grad, down_grad)

    def no_grads():
        return (
            jnp.zeros((normed_cols.shape[1], pre_grad_all.shape[1]), jnp.float32),
            jnp.zeros((hidden_all.shape[1], upstream_cols.shape[1]), jnp.float32),
        )

    up_grad, down_grad = lax.cond(jnp.logical_not(is_teacher), weight_grads, no_grads)
    return (generated, up_grad[None], down_grad[None])


def solution(mesh):
    in_specs = (
        P("rep", "tp"),
        P("rep", "tp"),
        P("rep", None),
        P("rep"),
        P(),
        P(None, "rep", "tp"),
        P(None, "tp", "rep"),
    )
    out_specs = (P("rep", "tp"), P("grp", "rep", "tp"), P("grp", "tp", "rep"))
    return jax.shard_map(body, mesh=mesh, in_specs=in_specs, out_specs=out_specs, check_vma=False)
```

profile of v0, /device:TPU:0, one launch (start us, length us, event | category | flops | bytes accessed | tf_op | source)
XLA Modules:
  0.0 1747.4 jit_solution(12708712042243029800)
XLA Ops:
  7.2 8.0 constant_dynamic-slice_fusion
  15.3 8.6 constant_dynamic-slice_fusion.1
  25.0 2.2 all_gather.27
  27.7 621.9 %all-gather.13.cloned.1.call-done = bf16[1,6144,3072]{2,1,0:T(8,128)(2,1)} async-done(((bf16[1,6144,768]{2,1,0:T(8,128)(2,1)}), bf16[1,6144,3072]{2,1,0:T(8,128)(2,1)}) %all-gather.13.cloned.1.call-update) | async-done | bytes 37748752 | tf_op jit(solution)/shard_map/all_gather | solution.py:76
  649.6 632.2 %all-gather.11.cloned.1.call-done = bf16[1,3072,6144]{2,1,0:T(8,128)(2,1)} async-done(((bf16[1,768,6144]{2,1,0:T(8,128)(2,1)}), bf16[1,3072,6144]{2,1,0:T(8,128)(2,1)}) %all-gather.11.cloned.1.call-update) | async-done | bytes 37748752 | tf_op jit(solution)/shard_map/all_gather | solution.py:75
  1281.8 31.9 %conditional.5 = (f32[64,6144]{1,0:T(8,128)S(1)}, bf16[64,6144]{1,0:T(8,128)(2,1)}, f32[64,3072]{1,0:T(8,128)S(1)}) conditional(s32[]{:T(128)} %convert_element_type.75, () %tuple.48, (bf16[64,3072]{1,0:T(8,128)(2,1)S(1)}, bf16[3072,6144]{1,0:T(8,128)(2,1)}, bf16[6144,3072]{1,0:T(8,128)(2,1)}) %tuple.98), branch_computations={%region_1.2_spmd, %region_2.3_spmd} | conditional | flops 4835377152 | bytes 79822872 | solution.py:38
  1281.8 16.6 fusion.7
  1298.4 15.3 fusion.49
  1315.4 5.3 reduce-scatter.3.cloned.1.call-done
  1321.8 12.6 all_gather.30
  1337.1 2.4 all_gather.31
  1341.0 3.6 conditional.6
  1345.9 37.4 %reduce-scatter.5.cloned.1.call-done = f32[128,1536]{1,0:T(8,128)} async-done(((f32[128,3072]{1,0:T(8,128)}), f32[128,1536]{1,0:T(8,128)}) %reduce-scatter.5.cloned.1.call-update) | async-done | bytes 786448 | tf_op jit(solution)/shard_map/reduce_scatter | solution.py:39
  1383.3 2.6 convert_select_fusion
  1388.8 59.7 %all-reduce.3.cloned.1.call-done = (f32[128,1536]{1,0:T(8,128)}, f32[128,1536]{1,0:T(8,128)}) async-done(((f32[128,1536]{1,0:T(8,128)}, f32[128,1536]{1,0:T(8,128)}), (f32[128,1536]{1,0:T(8,128)}, f32[128,1536]{1,0:T(8,128)})) %all-reduce.3.cloned.1.call-update) | async-done | bytes 1572880 | tf_op jit(solution)/shard_map/psum | solution.py:102
  1448.5 3.0 fusion.41
  1451.5 3.1 psum.23
  1456.4 2.1 all_gather.32
  1458.5 19.0 %conditional.7 = (bf16[64,6144]{1,0:T(8,128)(2,1)S(1)}) conditional(s32[]{:T(128)} %convert_element_type.75, () %tuple.51, (bf16[64,3072]{1,0:T(8,128)(2,1)S(1)}, bf16[6144,3072]{1,0:T(8,128)(2,1)}, f32[64,6144]{1,0:T(8,128)S(1)}) %tuple.96), branch_computations={%region_12.13_spmd, %region_13.14_spmd} | conditional | flops 2423783424 | bytes 40501256 | solution.py:52
  1458.5 19.0 %fusion.22 = bf16[64,6144]{1,0:T(8,128)(2,1)S(1)} fusion(f32[64,6144]{1,0:T(8,128)S(1)} %get-tuple-element.50, bf16[64,3072]{1,0:T(8,128)(2,1)S(1)} %get-tuple-element.48, bf16[6144,3072]{1,0:T(8,128)(2,1)} %get-tuple-element.49), kind=kOutput, calls=%fused_computation.26 | convolution fusion | flops 2423783424 | bytes 40501248 | tf_op jit(solution)/shard_map/cond/branch_1_fun/dot_general | solution.py:46
  1478.4 2.4 all_gather.33
  1484.0 2.1 copy.17
  1486.0 4.8 all-to-all-start
  1492.0 41.0 %all-to-all-done = bf16[128,4,768]{2,0,1:T(8,128)(2,1)S(1)} async-done(((bf16[128,4,768]{2,0,1:T(8,128)(2,1)}), bf16[128,4,768]{2,0,1:T(8,128)(2,1)S(1)}, u32[]{:S(2)}, u32[]{:S(2)}) %all-to-all-start) | async-done | bytes 786464 | tf_op jit(solution)/shard_map/all_to_all | solution.py:127
  1533.1 3.5 all-to-all-start.1
  1536.6 41.9 %all-to-all-done.1 = bf16[128,4,768]{2,0,1:T(8,128)(2,1)S(1)} async-done(((bf16[128,4,768]{2,0,1:T(8,128)(2,1)}), bf16[128,4,768]{2,0,1:T(8,128)(2,1)S(1)}, u32[]{:S(2)}, u32[]{:S(2)}) %all-to-all-start.1) | async-done | bytes 786464 | tf_op jit(solution)/shard_map/all_to_all | solution.py:128
  1578.5 20.9 %all-gather.9.cloned.1.call-done = bf16[512,6144]{1,0:T(8,128)(2,1)} async-done(((bf16[128,6144]{1,0:T(8,128)(2,1)}), bf16[512,6144]{1,0:T(8,128)(2,1)}) %all-gather.9.cloned.1.call-update) | async-done | bytes 6291472 | tf_op jit(solution)/shard_map/all_gather | solution.py:131
  1599.4 115.8 %all-gather.7.cloned.1.call-done = bf16[512,6144]{1,0:T(8,128)(2,1)} async-done(((bf16[128,6144]{1,0:T(8,128)(2,1)}), bf16[512,6144]{1,0:T(8,128)(2,1)}) %all-gather.7.cloned.1.call-update) | async-done | bytes 6291472 | tf_op jit(solution)/shard_map/all_gather | solution.py:132
  1715.2 18.5 %conditional.9 = (f32[1,768,6144]{2,1,0:T(8,128)}, f32[1,6144,768]{2,1,0:T(8,128)S(1)}) conditional(s32[]{:T(128)} %convert_element_type.80, () %tuple.50, (bf16[4,128,768]{2,1,0:T(8,128)(2,1)S(1)}, bf16[512,6144]{1,0:T(8,128)(2,1)}, bf16[4,128,768]{2,1,0:T(8,128)(2,1)S(1)}, bf16[512,6144]{1,0:T(8,128)(2,1)}) %tuple.101), branch_computations={%region_16.17_spmd, %region_17.18_spmd} | conditional | flops 9663676416 | bytes 80216208 | solution.py:146
  1716.3 7.8 convolution_bitcast_fusion
  1724.2 9.5 convolution_bitcast_fusion.1
  1733.7 6.8 copy-done.2
  (71 shorter events, 23.1 us)
Async XLA Ops:
  7.2 20.3 %copy-start = (f32[3,3072]{1,0:T(4,128)S(1)}, f32[3,3072]{1,0:T(4,128)}, u32[]{:S(2)}) copy-start(f32[3,3072]{1,0:T(4,128)} %param.21) | copy-start | bytes 110596
  7.2 642.4 %all-gather.13.cloned.1.call-start = ((), (), s32[]{:S(2)}) async-start(), calls=%async_computation.9 | async-start | bytes 47185920 | tf_op jit(solution)/shard_map/all_gather | solution.py:76
  15.3 1266.5 %all-gather.11.cloned.1.call-start = ((), (), s32[]{:S(2)}) async-start(), calls=%async_computation.8 | async-start | bytes 47185920 | tf_op jit(solution)/shard_map/all_gather | solution.py:75
  23.9 1.1 copy-start.12
  24.0 3.5 copy-start.13
  24.0 1296.7 %reduce-scatter.3.cloned.1.call-start = ((), (), s32[]{:S(2)}) async-start(), calls=%async_computation.4 | async-start | bytes 1179648 | tf_op jit(solution)/shard_map/reduce_scatter | solution.py:39
  1313.7 0.9 copy-start.7
  1314.6 68.6 %reduce-scatter.5.cloned.1.call-start = ((), (), s32[]{:S(2)}) async-start(), calls=%async_computation.5 | async-start | bytes 2359296 | tf_op jit(solution)/shard_map/reduce_scatter | solution.py:39
  1336.3 0.8 copy-start.4
  1344.6 1.1 copy-start.3
  1345.8 102.7 %all-reduce.3.cloned.1.call-start = ((), (), s32[]{:S(2)}) async-start(), calls=%async_computation.10 | async-start | bytes 3145728 | tf_op jit(solution)/shard_map/psum | solution.py:102
  1385.9 213.5 %all-gather.9.cloned.1.call-start = ((), (), s32[]{:S(2)}) async-start(), calls=%async_computation.7 | async-start | bytes 7864320 | tf_op jit(solution)/shard_map/all_gather | solution.py:131
  1387.2 61.3 %copy-start.9 = (bf16[128,1536]{1,0:T(8,128)(2,1)S(1)}, bf16[128,1536]{1,0:T(8,128)(2,1)}, u32[]{:S(2)}) copy-start(bf16[128,1536]{1,0:T(8,128)(2,1)} %get-tuple-element.84) | copy-start | bytes 1179652
  1388.8 326.4 %all-gather.7.cloned.1.call-start = ((), (), s32[]{:S(2)}) async-start(), calls=%async_computation.6 | async-start | bytes 7864320 | tf_op jit(solution)/shard_map/all_gather | solution.py:132
  1458.5 19.9 %copy-start.10 = (bf16[128,1536]{1,0:T(8,128)(2,1)S(1)}, bf16[128,1536]{1,0:T(8,128)(2,1)}, u32[]{:S(2)}) copy-start(bf16[128,1536]{1,0:T(8,128)(2,1)} %get-tuple-element.98) | copy-start | bytes 1179652
  1477.6 0.9 copy-start.8
  1486.0 47.0 %all-to-all-start = ((bf16[128,4,768]{2,0,1:T(8,128)(2,1)}), bf16[128,4,768]{2,0,1:T(8,128)(2,1)S(1)}, u32[]{:S(2)}, u32[]{:S(2)}) async-start(bf16[128,4,768]{2,0,1:T(8,128)(2,1)} %bitcast.38), calls=%async_computation.1 | async-start | bytes 1572864 | tf_op jit(solution)/shard_map/all_to_all | solution.py:127
  1533.1 45.5 %all-to-all-start.1 = ((bf16[128,4,768]{2,0,1:T(8,128)(2,1)}), bf16[128,4,768]{2,0,1:T(8,128)(2,1)S(1)}, u32[]{:S(2)}, u32[]{:S(2)}) async-start(bf16[128,4,768]{2,0,1:T(8,128)(2,1)} %bitcast.37), calls=%async_computation.3 | async-start | bytes 1572864 | tf_op jit(solution)/shard_map/all_to_all | solution.py:128
  1715.2 0.9 copy-start.5
  1715.2 1.1 copy-start.11
  1716.3 7.8 slice-start
  1716.3 7.8 slice-start.1
  1716.3 7.8 copy-start.6
  1733.7 6.8 copy-start.2
  1733.7 6.9 copy-start.1
Sparse Core Ops, SparseCore 0:
  15.4 634.1 all-gather.12
  651.8 630.0 all-gather.10
  1314.8 5.9 reduce-scatter.2
  1345.9 37.2 reduce-scatter.4
  1386.2 62.2 all-reduce.2
  1450.6 148.7 all-gather.8
  1601.6 113.4 all-gather.6
where the time goes:
time: 1750 us
  waiting for transfers between devices  1580 us (90%)
  matrix products  68.3 us (4%)
  local copies, waits for them, and re-layouts  36 us (2%)
  blocking collectives  24.7 us (1%)
  other arithmetic  17.6 us (1%)
    all_gather x1, waiting for transfers between devices, body(): lax.all_gather(own_up, 'rep', axis=0, tiled=True)  632 us
    all_gather x1, waiting for transfers between devices, body(): lax.all_gather(own_down, 'rep', axis=1, tiled=True)  622 us
    all_gather x1, waiting for transfers between devices, body(): lax.all_gather(pre_grad, 'rep', axis=0, tiled=True)  116 us
    psum x1, waiting for transfers between devices, body(): lax.psum((jnp.where(is_teacher, predicted, nothing), jnp.where(is_fake, p...  59.7 us
    reduce_scatter x2, waiting for transfers between devices, front_pass(): lax.psum_scatter(partial_terms, 'tp', scatter_dimension=1, tiled=True)  42.7 us
    all_to_all x1, waiting for transfers between devices, body(): lax.all_to_all(upstream, 'rep', split_axis=1, concat_axis=0, tiled=True)  41.9 us
    all_to_all x1, waiting for transfers between devices, body(): lax.all_to_all(normed, 'rep', split_axis=1, concat_axis=0, tiled=True)  41 us
  transfers between devices with their start and end apart: 9, of which 9 were waited for; matrix products, arithmetic and copies ran while one was open for 2% of the time, Pallas kernels for 0%

commit v1 on v0

v1 whole, which is shorter than its diff:
```python
import math

import jax
import jax.numpy as jnp
from jax import lax
from jax.sharding import PartitionSpec as P

IMG_TOK = 128
CHUNKS = 2
LOCKSTEP = True
F32 = jnp.float32
BF16 = jnp.bfloat16

INWARD = ((0, 1), (3, 2))
ACROSS = ((1, 2), (2, 1))
OUTWARD = ((1, 0), (2, 3))


def gelu_tanh(value):
    return jax.nn.gelu(value, approximate=True)


def dot(left, right):
    return jnp.dot(left, right, preferred_element_type=F32)


def dot_transposed(left, right):
    return lax.dot_general(left, right, (((1,), (1,)), ((), ())), preferred_element_type=F32)


def together(*tasks):
    tasks = list(tasks)
    results = [None] * len(tasks)
    inbox = [None] * len(tasks)
    active = list(range(len(tasks)))
    while active:
        sends, owners, still = [], [], []
        for i in active:
            try:
                messages = tasks[i].send(inbox[i])
            except StopIteration as stop:
                results[i] = stop.value
                continue
            owners.append((i, len(messages)))
            sends += messages
            still.append(i)
        active = still
        if not active:
            break
        received = yield sends
        at = 0
        for i, count in owners:
            inbox[i] = received[at : at + count]
            at += count
    return results


def delayed(rounds, task):
    for _ in range(rounds):
        yield []
    return (yield from task)


def drive(task):
    inbox, last = None, []
    while True:
        try:
            sends = task.send(inbox)
        except StopIteration as stop:
            return stop.value
        payloads = [payload for _, payload in sends]
        if LOCKSTEP and last and payloads:
            payloads, _ = lax.optimization_barrier((payloads, last))
        inbox = [lax.ppermute(v, "rep", pairs) for (pairs, _), v in zip(sends, payloads)]
        if inbox:
            last = inbox


def butterfly(value, axis):
    size = lax.axis_size(axis)
    step = 1
    while step < size:
        value = value + lax.ppermute(value, axis, [(i, i ^ step) for i in range(size)])
        step *= 2
    return value


def tp_sum(value):
    size = lax.axis_size("tp")
    if size == 2:
        return value + lax.ppermute(value, "tp", [(0, 1), (1, 0)])
    return lax.psum(value, "tp")


def reduce_line(partial):
    size = lax.axis_size("rep")
    if size != 4:
        return lax.psum(partial, "rep")
    lower = lax.axis_index("rep") < 2
    half = partial.shape[1] // 2
    low, high = partial[:, :half], partial[:, half:]
    first = jnp.where(lower, high, low)
    second = jnp.where(lower, low, high)
    (got,) = yield [(INWARD, first.astype(BF16))]
    (got,) = yield [(ACROSS, (first + got.astype(F32)).astype(BF16))]
    second = second + got.astype(F32)
    (got,) = yield [(OUTWARD, second.astype(BF16))]
    return second + got.astype(F32)


def spread_line(own):
    size = lax.axis_size("rep")
    if size != 4:
        return own
    index = lax.axis_index("rep")
    lower = index < 2
    end = (index == 0) | (index == 3)
    (got,) = yield [(INWARD, own)]
    second = jnp.where(end, own, got)
    (first_mid,) = yield [(ACROSS, second)]
    (first_end,) = yield [(OUTWARD, first_mid)]
    first = jnp.where(end, first_end, first_mid)
    return jnp.concatenate([jnp.where(lower, second, first), jnp.where(lower, first, second)], axis=1)


def forward(normed, factor, up, down):
    pre = yield from reduce_line(dot(normed, up))
    if factor is not None:
        pre = pre * factor
    hidden = yield from spread_line(gelu_tanh(pre).astype(BF16))
    return pre, hidden, tp_sum(dot(hidden, down))


def backward(upstream, scale, pre, down):
    grad = yield from reduce_line(dot_transposed(upstream, down))
    if scale is not None:
        grad = grad * scale
    pre_grad = jax.vjp(gelu_tanh, pre)[1](grad)[0].astype(BF16)
    return (yield from spread_line(pre_grad))


def body(noise_in, noise_renoise, text_cond, t_index, gains, up_weights, down_weights):
    g, r = lax.axis_index("grp"), lax.axis_index("rep")
    groups, reps = lax.axis_size("grp"), lax.axis_size("rep")
    rows = noise_in.shape[0]
    images = t_index.shape[0]
    n = rows // groups
    width = gains.shape[1]
    own_width = width // reps
    quarter = (g % 2) * (groups // 2) + g // 2
    image_of = (quarter * n + jnp.arange(n)) // IMG_TOK

    def mine(whole):
        return lax.dynamic_slice_in_dim(whole, quarter * n, n, 0)

    both = jnp.concatenate([mine(noise_in), mine(noise_renoise)], axis=0)
    both = lax.all_gather(both, "tp", axis=1, tiled=True)
    values = both[:n].astype(F32)
    cond = text_cond.astype(F32)
    cond_rows = jnp.broadcast_to(cond, (n, width)) if images == 1 else jnp.take(cond, image_of, axis=0)
    factor = lax.rsqrt(jnp.mean(values * values, axis=-1, keepdims=True) + 1e-06)
    normed = (values * factor * gains[0][None, :] * (1.0 + cond_rows)).astype(BF16)
    normed = lax.all_to_all(normed, "rep", split_axis=1, concat_axis=0, tiled=True)

    high = (t_index // 256).astype(BF16)
    low = (t_index % 256).astype(BF16)
    extra = 3 * images
    pad = -(2 * n + extra) % 16
    side = jnp.concatenate(
        [
            both,
            text_cond,
            jnp.broadcast_to(high[:, None], (images, width)),
            jnp.broadcast_to(low[:, None], (images, width)),
            jnp.zeros((pad, width), BF16),
        ],
        axis=0,
    )
    side = lax.all_to_all(side, "rep", split_axis=1, concat_axis=0, tiled=True)
    side = side.reshape(reps, 2 * n + extra + pad, own_width)

    def per_row(block):
        if images == 1:
            spread = jnp.broadcast_to(block, (reps, n, block.shape[-1]))
        else:
            spread = jnp.take(block, image_of, axis=1)
        return spread.reshape(reps * n, block.shape[-1])

    at = 2 * n
    x_in = side[:, :n].reshape(reps * n, own_width)
    renoise = side[:, n:at].reshape(reps * n, own_width)
    cond_part = 1.0 + per_row(side[:, at : at + images].astype(F32))
    steps = side[:, at + images : at + 3 * images, :1].astype(F32)
    t_values = steps[:, :images] * 256.0 + steps[:, images:]
    sigma = per_row(0.1 + 0.8 * t_values / 999.0)
    own_gains = lax.dynamic_slice_in_dim(gains, r * own_width, own_width, 1)

    total = reps * n
    push_scale = 1.0 / math.sqrt(rows * reps)
    image_rows = jnp.repeat(jnp.arange(reps), n) * images + jnp.tile(image_of, reps)

    def image_sums(part):
        count = part.shape[0] // n
        if images == 1:
            sums = butterfly(butterfly(jnp.sum(part.reshape(count, n), axis=1), "rep"), "grp")
            return jnp.repeat(sums, n)[:, None]
        hot = (image_rows[:, None] == jnp.arange(reps * images)[None, :]).astype(F32)
        hot = hot[: part.shape[0]]
        sums = butterfly(butterfly(jnp.sum(part[:, None] * hot, axis=0), "rep"), "grp")
        return jnp.sum(hot * sums[None, :], axis=1, keepdims=True)

    def chain(at, count):
        def cut(whole):
            return whole[at : at + count]

        x, cond_1, sig = cut(x_in).astype(F32), cut(cond_part), cut(sigma)
        pre_s, hidden_s, out = yield from forward(cut(normed), None, up_weights[0], down_weights[0])
        made = (x + out).astype(BF16)
        made_f = made.astype(F32)
        noised = ((1.0 - sig) * made_f + sig * cut(renoise).astype(F32)).astype(BF16)
        noised_f = noised.astype(F32)
        squares = butterfly(jnp.sum(noised_f * noised_f, axis=1), "rep")[:, None]
        factor = lax.rsqrt(squares / width + 1e-06)
        scaled = noised_f * cond_1
        teacher = forward((scaled * own_gains[1][None, :]).astype(BF16), factor, up_weights[1], down_weights[1])
        fake = forward((scaled * own_gains[2][None, :]).astype(BF16), factor, up_weights[2], down_weights[2])
        (_, _, out_t), (pre_f, hidden_f, out_f) = yield from together(teacher, delayed(1, fake))
        real_f = (noised_f + out_t).astype(BF16).astype(F32)
        fake_f = (noised_f + out_f).astype(BF16).astype(F32)
        push_f = ((fake_f - made_f) * push_scale).astype(BF16)
        raw_s = (fake_f - real_f) * push_scale
        distance = image_sums(jnp.sum(jnp.abs(made_f - real_f), axis=1))
        inverse = 1.0 / (distance / (IMG_TOK * width) + 1e-05)
        grad_f, grad_s = yield from together(
            backward(push_f, None, pre_f, down_weights[2]),
            delayed(1, backward(raw_s.astype(BF16), inverse, pre_s, down_weights[0])),
        )
        push_s = (raw_s * inverse).astype(BF16)
        normed_f = (noised_f * factor * own_gains[2][None, :] * cond_1).astype(BF16)
        return made, (cut(normed), push_s, hidden_s, grad_s), (normed_f, push_f, hidden_f, grad_f)

    chunks = CHUNKS if images == 1 and reps % CHUNKS == 0 else 1
    count = total // chunks
    parts = drive(together(*[delayed(2 * c, chain(c * count, count)) for c in range(chunks)]))

    made = jnp.concatenate([p[0] for p in parts], axis=0)
    made = lax.all_to_all(made, "rep", split_axis=0, concat_axis=1, tiled=True)
    tp_width = noise_in.shape[1]
    made = lax.dynamic_slice_in_dim(made, lax.axis_index("tp") * tp_width, tp_width, 1)
    made = lax.all_gather(made, "grp", axis=0)
    generated = jnp.concatenate([made[i] for i in (0, 2, 1, 3)], axis=0)

    is_fake = g == 3
    keep = g != 2

    def gather_rows(student, fake, masked):
        own = jnp.where(is_fake, fake, student)
        if masked:
            own = jnp.where(keep, own, jnp.zeros_like(own))
        from_y = jnp.where(
            is_fake,
            lax.ppermute(fake, "grp", ((1, 3),)),
            lax.ppermute(student, "grp", ((2, 0), (3, 1))),
        )
        from_x = lax.ppermute(fake, "grp", ((2, 3),))
        from_d = lax.ppermute(fake, "grp", ((0, 3),))
        return [own, from_y, from_x, from_d]

    gathered = []
    for k in range(4):
        blocks = []
        for _, student, fake in parts:
            blocks += gather_rows(student[k], fake[k], k < 2)
        gathered.append(jnp.concatenate(blocks, axis=0))
    normed_all, push_all, hidden_all, grad_all = gathered
    down_grad = dot(hidden_all.T, push_all)
    up_grad = dot(normed_all.T, grad_all)
    return (generated, up_grad[None], down_grad[None])


def solution(mesh):
    in_specs = (
        P("rep", "tp"),
        P("rep", "tp"),
        P("rep", None),
        P("rep"),
        P(),
        P(None, "rep", "tp"),
        P(None, "tp", "rep"),
    )
    out_specs = (P("rep", "tp"), P("grp", "rep", "tp"), P("grp", "tp", "rep"))
    return jax.shard_map(body, mesh=mesh, in_specs=in_specs, out_specs=out_specs, check_vma=False)
```

time: 1750 us -> 699 us (0.40)
  waiting for transfers between devices: 1580 us -> 211 us
  starting transfers between devices: 8.54 us -> 284 us
  matrix products: 68.3 us -> 114 us
  other arithmetic: 17.6 us -> 45.9 us
  local copies, waits for them, and re-layouts: 36 us -> 17 us
    all_gather x4 -> x0, waiting for transfers between devices: 1390 us -> none  [the longest x1 632 us: body(): lax.all_gather(own_up, 'rep', axis=0, tiled=True)]
    ppermute x0 -> x110, starting transfers between devices: none -> 270 us  [the longest x60 182 us: drive(): lax.ppermute(v, 'rep', pairs)]
    ppermute x0 -> x110, waiting for transfers between devices: none -> 203 us  [the longest x60 143 us: drive(): lax.ppermute(v, 'rep', pairs)]
    psum x1 -> x0, waiting for transfers between devices: 59.7 us -> none  [body(): lax.psum((jnp.where(is_teacher, predicted, nothing), jnp.where(is_fake, p...]
    dot_general x5 -> x18, matrix products: 68.3 us -> 114 us  [the longest x14 87.4 us: dot(): return jnp.dot(left, right, preferred_element_type=F32)]
    reduce_scatter x2 -> x0, waiting for transfers between devices: 42.7 us -> none  [front_pass(): lax.psum_scatter(partial_terms, 'tp', scatter_dimension=1, tiled=True)]
    all_to_all x1 -> x2, waiting for transfers between devices: 41.9 us -> 0.01 us  [the longest x1 0.01 us: body(): side = lax.all_to_all(side, 'rep', split_axis=1, concat_axis=0, tiled=True)]
    all_to_all x1, waiting for transfers between devices: 41 us -> 7.82 us  [body(): lax.all_to_all(normed, 'rep', split_axis=1, concat_axis=0, tiled=True)]
  transfers between devices with their start and end apart: 9 -> 113, of which waited for: 9 -> 44; matrix products, arithmetic and copies ran while one was open for 2% -> 22% of each run, Pallas kernels for 0% -> 0%
where the time goes in v1:
time: 699 us; the launch traced here: 686 us
  starting transfers between devices  284 us (41%)
  waiting for transfers between devices  211 us (30%)
  matrix products  114 us (16%)
  other arithmetic  45.9 us (7%)
  local copies, waits for them, and re-layouts  17 us (2%)
  blocking collectives  10.2 us (1%)
    ppermute x60, starting transfers between devices, drive(): lax.ppermute(v, 'rep', pairs)  182 us
    ppermute x60, waiting for transfers between devices, drive(): lax.ppermute(v, 'rep', pairs)  143 us
    dot_general x14, matrix products, dot(): return jnp.dot(left, right, preferred_element_type=F32)  87.4 us
    ppermute x8, starting transfers between devices, gather_rows(): from_d = lax.ppermute(fake, 'grp', ((0, 3),))  48.5 us
    ppermute x12, waiting for transfers between devices, butterfly(): lax.ppermute(value, axis, [(i, i ^ step) for i in range(size)])  29.2 us
    dot_general x4, matrix products, dot_transposed(): lax.dot_general(left, right, (((1,), (1,)), ((), ())), preferred_element_...  26.6 us
    ppermute x8, waiting for transfers between devices, gather_rows(): from_d = lax.ppermute(fake, 'grp', ((0, 3),))  22.7 us
    ppermute x12, starting transfers between devices, butterfly(): lax.ppermute(value, axis, [(i, i ^ step) for i in range(size)])  16.1 us
  transfers between devices with their start and end apart: 113, of which 44 were waited for; matrix products, arithmetic and copies ran while one was open for 22% of the time, Pallas kernels for 0%

profile of v1, /device:TPU:0, one launch (start us, length us, event | category | flops | bytes accessed | tf_op | source)
XLA Modules:
  0.0 686.4 jit_solution(12782973252456212840)
XLA Ops:
  12.6 7.8 %all-to-all-done.1 = bf16[32,4,768]{2,0,1:T(8,128)(2,1)S(1)} async-done(((bf16[32,4,768]{2,0,1:T(8,128)(2,1)}), bf16[32,4,768]{2,0,1:T(8,128)(2,1)S(1)}, u32[]{:S(2)}, u32[]{:S(2)}) %all-to-all-start.1) | async-done | bytes 196640 | tf_op jit(solution)/shard_map/all_to_all | solution.py:163
  38.1 14.3 %collective-permute-start.3 = (bf16[64,3072]{1,0:T(8,128)(2,1)}, bf16[64,3072]{1,0:T(8,128)(2,1)}, u32[]{:S(2)}, u32[]{:S(2)}) collective-permute-start(bf16[64,3072]{1,0:T(8,128)(2,1)} %fusion.103), channel_id=1, source_target_pairs={{0,2},{6,4},{1,3},{7,5},{8,10},{14,12},{9,11},{15,13},{16,18},{22,... | collective-permute-start | bytes 1179656 | tf_op jit(solution)/shard_map/ppermute | solution.py:74
  61.2 12.9 %collective-permute-done.2 = bf16[64,3072]{1,0:T(8,128)(2,1)S(1)} collective-permute-done((bf16[64,3072]{1,0:T(8,128)(2,1)}, bf16[64,3072]{1,0:T(8,128)(2,1)S(1)}, u32[]{:S(2)}, u32[]{:S(2)}) %collective-permute-start.2) | collective-permute-done | bytes 393248 | tf_op jit(solution)/shard_map/ppermute | solution.py:74
  102.3 9.6 %collective-permute-done.8 = bf16[64,3072]{1,0:T(8,128)(2,1)S(1)} collective-permute-done((bf16[64,3072]{1,0:T(8,128)(2,1)S(1)}, bf16[64,3072]{1,0:T(8,128)(2,1)S(1)}, u32[]{:S(2)}, u32[]{:S(2)}) %collective-permute-start.8) | collective-permute-done | bytes 393248 | tf_op jit(solution)/shard_map/ppermute | solution.py:74
  120.3 8.2 %collective-permute-done.15 = f32[64]{0:T(128)S(1)} collective-permute-done((f32[64]{0:T(128)S(1)}, f32[64]{0:T(128)S(1)}, u32[]{:S(2)}, u32[]{:S(2)}) %collective-permute-start.15) | collective-permute-done | bytes 288 | tf_op jit(solution)/shard_map/ppermute | solution.py:83
  152.5 7.7 %collective-permute-start.20 = (bf16[64,768]{1,0:T(8,128)(2,1)S(1)}, bf16[64,768]{1,0:T(8,128)(2,1)S(1)}, u32[]{:S(2)}, u32[]{:S(2)}) collective-permute-start(bf16[64,768]{1,0:T(8,128)(2,1)S(1)} %get-tuple-element.193), channel_id=1, source_target_pairs={{0,24},{1,25},{2,26},{3,27},{4,28},{5,29},{6,30},{7,31}} | collective-permute-start | bytes 294920 | tf_op jit(solution)/shard_map/ppermute | solution.py:266
  164.3 14.6 %collective-permute-start.28 = (bf16[64,3072]{1,0:T(8,128)(2,1)S(1)}, bf16[64,3072]{1,0:T(8,128)(2,1)S(1)}, u32[]{:S(2)}, u32[]{:S(2)}) collective-permute-start(bf16[64,3072]{1,0:T(8,128)(2,1)S(1)} %fusion.105), channel_id=1, source_target_pairs={{0,2},{6,4},{1,3},{7,5},{8,10},{14,12},{9,11},{15,13},{16,18},{22,... | collective-permute-start | bytes 1179656 | tf_op jit(solution)/shard_map/ppermute | solution.py:74
  215.5 9.2 %collective-permute-start.31 = (bf16[64,3072]{1,0:T(8,128)(2,1)S(1)}, bf16[64,3072]{1,0:T(8,128)(2,1)S(1)}, u32[]{:S(2)}, u32[]{:S(2)}) collective-permute-start(bf16[64,3072]{1,0:T(8,128)(2,1)S(1)} %fusion.106), channel_id=1, source_target_pairs={{0,2},{6,4},{1,3},{7,5},{8,10},{14,12},{9,11},{15,13},{16,18},{22,... | collective-permute-start | bytes 1179656 | tf_op jit(solution)/shard_map/ppermute | solution.py:74
  224.9 7.1 %collective-permute-done.31 = bf16[64,3072]{1,0:T(8,128)(2,1)S(1)} collective-permute-done((bf16[64,3072]{1,0:T(8,128)(2,1)S(1)}, bf16[64,3072]{1,0:T(8,128)(2,1)S(1)}, u32[]{:S(2)}, u32[]{:S(2)}) %collective-permute-start.31) | collective-permute-done | bytes 393248 | tf_op jit(solution)/shard_map/ppermute | solution.py:74
  233.4 9.4 %collective-permute-done.30 = bf16[64,3072]{1,0:T(8,128)(2,1)S(1)} collective-permute-done((bf16[64,3072]{1,0:T(8,128)(2,1)S(1)}, bf16[64,3072]{1,0:T(8,128)(2,1)S(1)}, u32[]{:S(2)}, u32[]{:S(2)}) %collective-permute-start.30) | collective-permute-done | bytes 393248 | tf_op jit(solution)/shard_map/ppermute | solution.py:74
  269.6 8.0 %all-gather = bf16[128,1536]{1,0:T(8,128)(2,1)S(1)} all-gather(bf16[32,1536]{1,0:T(8,128)(2,1)S(1)} %constant_dynamic-slice_fusion), channel_id=2, replica_groups=mesh['grp'=4,'rep'=4,'tp'=2] {'grp'}, dimensions={0}, use_global_device_ids=true | all-gather | bytes 491520 | tf_op jit(solution)/shard_map/all_gather | solution.py:250
  349.8 6.6 fusion.8
  357.2 6.6 fusion.22
  366.0 8.8 %collective-permute-start.97 = (bf16[64,6144]{1,0:T(8,128)(2,1)}, bf16[64,6144]{1,0:T(8,128)(2,1)}, u32[]{:S(2)}, u32[]{:S(2)}) collective-permute-start(bf16[64,6144]{1,0:T(8,128)(2,1)} %get-tuple-element.176), channel_id=1, source_target_pairs={{0,24},{1,25},{2,26},{3,27},{4,28},{5,29},{6,30},{7,31}} | collective-permute-start | bytes 2359304 | tf_op jit(solution)/shard_map/ppermute | solution.py:266
  381.7 11.3 %collective-permute-done.105 = bf16[64,768]{1,0:T(8,128)(2,1)S(1)} collective-permute-done((bf16[64,768]{1,0:T(8,128)(2,1)S(1)}, bf16[64,768]{1,0:T(8,128)(2,1)S(1)}, u32[]{:S(2)}, u32[]{:S(2)}) %collective-permute-start.105) | collective-permute-done | bytes 98336 | tf_op jit(solution)/shard_map/ppermute | solution.py:266
  397.9 8.9 %collective-permute-done.51 = bf16[64,3072]{1,0:T(8,128)(2,1)S(1)} collective-permute-done((bf16[64,3072]{1,0:T(8,128)(2,1)}, bf16[64,3072]{1,0:T(8,128)(2,1)S(1)}, u32[]{:S(2)}, u32[]{:S(2)}) %collective-permute-start.51) | collective-permute-done | bytes 393248 | tf_op jit(solution)/shard_map/ppermute | solution.py:74
  416.9 11.7 %collective-permute-start.53 = (bf16[64,3072]{1,0:T(8,128)(2,1)}, bf16[64,3072]{1,0:T(8,128)(2,1)}, u32[]{:S(2)}, u32[]{:S(2)}) collective-permute-start(bf16[64,3072]{1,0:T(8,128)(2,1)} %fusion.109), channel_id=1, source_target_pairs={{0,2},{6,4},{1,3},{7,5},{8,10},{14,12},{9,11},{15,13},{16,18},{22,... | collective-permute-start | bytes 1179656 | tf_op jit(solution)/shard_map/ppermute | solution.py:74
  465.5 6.6 fusion.4
  472.1 6.7 fusion.20
  480.3 12.0 %collective-permute-done.56 = bf16[64,3072]{1,0:T(8,128)(2,1)S(1)} collective-permute-done((bf16[64,3072]{1,0:T(8,128)(2,1)S(1)}, bf16[64,3072]{1,0:T(8,128)(2,1)S(1)}, u32[]{:S(2)}, u32[]{:S(2)}) %collective-permute-start.56) | collective-permute-done | bytes 393248 | tf_op jit(solution)/shard_map/ppermute | solution.py:74
  509.7 15.2 %collective-permute-start.67 = (bf16[64,3072]{1,0:T(8,128)(2,1)S(1)}, bf16[64,3072]{1,0:T(8,128)(2,1)S(1)}, u32[]{:S(2)}, u32[]{:S(2)}) collective-permute-start(bf16[64,3072]{1,0:T(8,128)(2,1)S(1)} %fusion.111), channel_id=1, source_target_pairs={{0,2},{6,4},{1,3},{7,5},{8,10},{14,12},{9,11},{15,13},{16,18},{22,... | collective-permute-start | bytes 1179656 | tf_op jit(solution)/shard_map/ppermute | solution.py:74
  531.2 13.1 %collective-permute-start.60 = (bf16[64,3072]{1,0:T(8,128)(2,1)S(1)}, bf16[64,3072]{1,0:T(8,128)(2,1)S(1)}, u32[]{:S(2)}, u32[]{:S(2)}) collective-permute-start(bf16[64,3072]{1,0:T(8,128)(2,1)S(1)} %fusion.68), channel_id=1, source_target_pairs={{0,2},{6,4},{1,3},{7,5},{8,10},{14,12},{9,11},{15,13},{16,18},{22,... | collective-permute-start | bytes 1179656 | tf_op jit(solution)/shard_map/ppermute | solution.py:74
  550.9 9.6 %collective-permute-done.61 = bf16[64,3072]{1,0:T(8,128)(2,1)S(1)} collective-permute-done((bf16[64,3072]{1,0:T(8,128)(2,1)S(1)}, bf16[64,3072]{1,0:T(8,128)(2,1)S(1)}, u32[]{:S(2)}, u32[]{:S(2)}) %collective-permute-start.61) | collective-permute-done | bytes 393248 | tf_op jit(solution)/shard_map/ppermute | solution.py:74
  563.7 7.0 %collective-permute-start.69 = (bf16[64,3072]{1,0:T(8,128)(2,1)S(1)}, bf16[64,3072]{1,0:T(8,128)(2,1)S(1)}, u32[]{:S(2)}, u32[]{:S(2)}) collective-permute-start(bf16[64,3072]{1,0:T(8,128)(2,1)S(1)} %fusion.54), channel_id=1, source_target_pairs={{0,2},{6,4},{1,3},{7,5},{8,10},{14,12},{9,11},{15,13},{16,18},{22,... | collective-permute-start | bytes 1179656 | tf_op jit(solution)/shard_map/ppermute | solution.py:74
  604.5 8.0 %collective-permute-done.80 = bf16[64,3072]{1,0:T(8,128)(2,1)S(1)} collective-permute-done((bf16[64,3072]{1,0:T(8,128)(2,1)S(1)}, bf16[64,3072]{1,0:T(8,128)(2,1)S(1)}, u32[]{:S(2)}, u32[]{:S(2)}) %collective-permute-start.80) | collective-permute-done | bytes 393248 | tf_op jit(solution)/shard_map/ppermute | solution.py:74
  617.6 7.1 %collective-permute-done.87 = bf16[64,3072]{1,0:T(8,128)(2,1)S(1)} collective-permute-done((bf16[64,3072]{1,0:T(8,128)(2,1)S(1)}, bf16[64,3072]{1,0:T(8,128)(2,1)S(1)}, u32[]{:S(2)}, u32[]{:S(2)}) %collective-permute-start.87) | collective-permute-done | bytes 393248 | tf_op jit(solution)/shard_map/ppermute | solution.py:74
  624.7 8.9 %collective-permute-start.84 = (bf16[64,6144]{1,0:T(8,128)(2,1)S(1)}, bf16[64,6144]{1,0:T(8,128)(2,1)S(1)}, u32[]{:S(2)}, u32[]{:S(2)}) collective-permute-start(bf16[64,6144]{1,0:T(8,128)(2,1)S(1)} %get-tuple-element.182), channel_id=1, source_target_pairs={{0,24},{1,25},{2,26},{3,27},{4,28},{5,29},{6,30},{7,31}} | collective-permute-start | bytes 2359304 | tf_op jit(solution)/shard_map/ppermute | solution.py:266
  635.2 8.0 %collective-permute-done.89 = bf16[64,3072]{1,0:T(8,128)(2,1)S(1)} collective-permute-done((bf16[64,3072]{1,0:T(8,128)(2,1)S(1)}, bf16[64,3072]{1,0:T(8,128)(2,1)S(1)}, u32[]{:S(2)}, u32[]{:S(2)}) %collective-permute-start.89) | collective-permute-done | bytes 393248 | tf_op jit(solution)/shard_map/ppermute | solution.py:74
  645.9 9.5 %convolution_bitcast_fusion = f32[1,6144,768]{2,1,0:T(8,128)} fusion(bf16[512,6144]{1,0:T(8,128)(2,1)S(1)} %constant_dynamic-update-slice_fusion.8, bf16[512,768]{1,0:T(8,128)(2,1)S(1)} %constant_dynamic-update-slice_fusion.12), kind=kOutput, calls=%fused_computation | convolution fusion | flops 4831838208 | bytes 25952256 | tf_op jit(solution)/shard_map/dot_general | solution.py:24
  656.1 9.6 %collective-permute-start.93 = (bf16[64,6144]{1,0:T(8,128)(2,1)S(1)}, bf16[64,6144]{1,0:T(8,128)(2,1)S(1)}, u32[]{:S(2)}, u32[]{:S(2)}) collective-permute-start(bf16[64,6144]{1,0:T(8,128)(2,1)S(1)} %get-tuple-element.179), channel_id=1, source_target_pairs={{0,24},{1,25},{2,26},{3,27},{4,28},{5,29},{6,30},{7,31}} | collective-permute-start | bytes 2359304 | tf_op jit(solution)/shard_map/ppermute | solution.py:266
  666.0 9.2 %collective-permute-done.93 = bf16[64,6144]{1,0:T(8,128)(2,1)S(1)} collective-permute-done((bf16[64,6144]{1,0:T(8,128)(2,1)S(1)}, bf16[64,6144]{1,0:T(8,128)(2,1)S(1)}, u32[]{:S(2)}, u32[]{:S(2)}) %collective-permute-start.93) | collective-permute-done | bytes 786464 | tf_op jit(solution)/shard_map/ppermute | solution.py:266
  675.3 10.7 %convolution_bitcast_fusion.1 = f32[1,768,6144]{2,1,0:T(8,128)} fusion(bf16[512,768]{1,0:T(8,128)(2,1)} %constant_dynamic-update-slice_fusion, bf16[512,6144]{1,0:T(8,128)(2,1)S(1)} %constant_dynamic-update-slice_fusion.4), kind=kOutput, calls=%fused_computation.1 | convolution fusion | flops 4831838208 | bytes 25952256 | tf_op jit(solution)/shard_map/dot_general | solution.py:24
  (466 shorter events, 378.4 us)
Async XLA Ops:
  38.1 21.2 %collective-permute-start.3 = (bf16[64,3072]{1,0:T(8,128)(2,1)}, bf16[64,3072]{1,0:T(8,128)(2,1)}, u32[]{:S(2)}, u32[]{:S(2)}) collective-permute-start(bf16[64,3072]{1,0:T(8,128)(2,1)} %fusion.103), channel_id=1, source_target_pairs={{0,2},{6,4},{1,3},{7,5},{8,10},{14,12},{9,11},{15,13},{16,18},{22,... | collective-permute-start | bytes 1179656 | tf_op jit(solution)/shard_map/ppermute | solution.py:74
  54.4 25.7 %all-to-all-start = ((bf16[80,4,768]{2,0,1:T(8,128)(2,1)}), bf16[80,4,768]{2,0,1:T(8,128)(2,1)S(1)}, u32[]{:S(2)}, u32[]{:S(2)}) async-start(bf16[80,4,768]{2,0,1:T(8,128)(2,1)} %bitcast.118), calls=%async_computation | async-start | bytes 983040 | tf_op jit(solution)/shard_map/all_to_all | solution.py:179
  77.5 82.7 %collective-permute-start.18 = (bf16[64,768]{1,0:T(8,128)(2,1)}, bf16[64,768]{1,0:T(8,128)(2,1)}, u32[]{:S(2)}, u32[]{:S(2)}) collective-permute-start(bf16[64,768]{1,0:T(8,128)(2,1)} %bitcast.130), channel_id=1, source_target_pairs={{16,0},{24,8},{17,1},{25,9},{18,2},{26,10},{19,3},{27,11},{20,4},{... | collective-permute-start | bytes 294920 | tf_op jit(solution)/shard_map/ppermute | solution.py:263
  78.8 166.5 %collective-permute-start.24 = (bf16[64,768]{1,0:T(8,128)(2,1)}, bf16[64,768]{1,0:T(8,128)(2,1)}, u32[]{:S(2)}, u32[]{:S(2)}) collective-permute-start(bf16[64,768]{1,0:T(8,128)(2,1)} %bitcast.127), channel_id=1, source_target_pairs={{16,0},{24,8},{17,1},{25,9},{18,2},{26,10},{19,3},{27,11},{20,4},{... | collective-permute-start | bytes 294920 | tf_op jit(solution)/shard_map/ppermute | solution.py:263
  133.6 27.9 %collective-permute-start.17 = (bf16[64,768]{1,0:T(8,128)(2,1)S(1)}, bf16[64,768]{1,0:T(8,128)(2,1)S(1)}, u32[]{:S(2)}, u32[]{:S(2)}) collective-permute-start(bf16[64,768]{1,0:T(8,128)(2,1)S(1)} %get-tuple-element.193), channel_id=1, source_target_pairs={{8,24},{9,25},{10,26},{11,27},{12,28},{13,29},{14,30},{15,31}} | collective-permute-start | bytes 294920 | tf_op jit(solution)/shard_map/ppermute | solution.py:262
  134.3 28.8 %collective-permute-start.19 = (bf16[64,768]{1,0:T(8,128)(2,1)S(1)}, bf16[64,768]{1,0:T(8,128)(2,1)S(1)}, u32[]{:S(2)}, u32[]{:S(2)}) collective-permute-start(bf16[64,768]{1,0:T(8,128)(2,1)S(1)} %get-tuple-element.193), channel_id=1, source_target_pairs={{16,24},{17,25},{18,26},{19,27},{20,28},{21,29},{22,30},{23,31}} | collective-permute-start | bytes 294920 | tf_op jit(solution)/shard_map/ppermute | solution.py:265
  164.3 21.2 %collective-permute-start.28 = (bf16[64,3072]{1,0:T(8,128)(2,1)S(1)}, bf16[64,3072]{1,0:T(8,128)(2,1)S(1)}, u32[]{:S(2)}, u32[]{:S(2)}) collective-permute-start(bf16[64,3072]{1,0:T(8,128)(2,1)S(1)} %fusion.105), channel_id=1, source_target_pairs={{0,2},{6,4},{1,3},{7,5},{8,10},{14,12},{9,11},{15,13},{16,18},{22,... | collective-permute-start | bytes 1179656 | tf_op jit(solution)/shard_map/ppermute | solution.py:74
  197.8 70.8 %all-to-all-start.2 = ((bf16[4,32,768]{2,1,0:T(8,128)(2,1)}), bf16[4,32,768]{2,1,0:T(8,128)(2,1)}, u32[]{:S(2)}, u32[]{:S(2)}) async-start(bf16[4,32,768]{2,1,0:T(8,128)(2,1)} %bitcast.16), calls=%async_computation.2 | async-start | bytes 393216 | tf_op jit(solution)/shard_map/all_to_all | solution.py:247
  209.1 36.2 %collective-permute-start.23 = (bf16[64,768]{1,0:T(8,128)(2,1)S(1)}, bf16[64,768]{1,0:T(8,128)(2,1)S(1)}, u32[]{:S(2)}, u32[]{:S(2)}) collective-permute-start(bf16[64,768]{1,0:T(8,128)(2,1)S(1)} %get-tuple-element.196), channel_id=1, source_target_pairs={{8,24},{9,25},{10,26},{11,27},{12,28},{13,29},{14,30},{15,31}} | collective-permute-start | bytes 294920 | tf_op jit(solution)/shard_map/ppermute | solution.py:262
  209.8 37.1 %collective-permute-start.25 = (bf16[64,768]{1,0:T(8,128)(2,1)S(1)}, bf16[64,768]{1,0:T(8,128)(2,1)S(1)}, u32[]{:S(2)}, u32[]{:S(2)}) collective-permute-start(bf16[64,768]{1,0:T(8,128)(2,1)S(1)} %get-tuple-element.196), channel_id=1, source_target_pairs={{16,24},{17,25},{18,26},{19,27},{20,28},{21,29},{22,30},{23,31}} | collective-permute-start | bytes 294920 | tf_op jit(solution)/shard_map/ppermute | solution.py:265
  210.4 57.5 %collective-permute-start.26 = (bf16[64,768]{1,0:T(8,128)(2,1)S(1)}, bf16[64,768]{1,0:T(8,128)(2,1)S(1)}, u32[]{:S(2)}, u32[]{:S(2)}) collective-permute-start(bf16[64,768]{1,0:T(8,128)(2,1)S(1)} %get-tuple-element.196), channel_id=1, source_target_pairs={{0,24},{1,25},{2,26},{3,27},{4,28},{5,29},{6,30},{7,31}} | collective-permute-start | bytes 294920 | tf_op jit(solution)/shard_map/ppermute | solution.py:266
  311.0 27.1 %collective-permute-start.44 = (bf16[64,3072]{1,0:T(8,128)(2,1)S(1)}, bf16[64,3072]{1,0:T(8,128)(2,1)}, u32[]{:S(2)}, u32[]{:S(2)}) collective-permute-start(bf16[64,3072]{1,0:T(8,128)(2,1)S(1)} %collective-permute-done.40), channel_id=1, source_target_pairs={{2,0},{4,6},{3,1},{5,7},{10,8},{12,14},{11,9},{13,15},{18,16},{20,... | collective-permute-start | bytes 1179656 | tf_op jit(solution)/shard_map/ppermute | solution.py:74
  312.3 36.0 %collective-permute-start.47 = (bf16[64,3072]{1,0:T(8,128)(2,1)S(1)}, bf16[64,3072]{1,0:T(8,128)(2,1)}, u32[]{:S(2)}, u32[]{:S(2)}) collective-permute-start(bf16[64,3072]{1,0:T(8,128)(2,1)S(1)} %multiply_convert_fusion), channel_id=1, source_target_pairs={{0,2},{6,4},{1,3},{7,5},{8,10},{14,12},{9,11},{15,13},{16,18},{22,... | collective-permute-start | bytes 1179656 | tf_op jit(solution)/shard_map/ppermute | solution.py:74
  318.3 47.6 %collective-permute-start.46 = (bf16[64,3072]{1,0:T(8,128)(2,1)}, bf16[64,3072]{1,0:T(8,128)(2,1)}, u32[]{:S(2)}, u32[]{:S(2)}) collective-permute-start(bf16[64,3072]{1,0:T(8,128)(2,1)} %broadcast_select_fusion.13), channel_id=1, source_target_pairs={{2,4},{4,2},{3,5},{5,3},{10,12},{12,10},{11,13},{13,11},{18,20},{2... | collective-permute-start | bytes 1179656 | tf_op jit(solution)/shard_map/ppermute | solution.py:74
  340.5 74.1 %collective-permute-start.94 = (bf16[64,6144]{1,0:T(8,128)(2,1)}, bf16[64,6144]{1,0:T(8,128)(2,1)S(1)}, u32[]{:S(2)}, u32[]{:S(2)}) collective-permute-start(bf16[64,6144]{1,0:T(8,128)(2,1)} %get-tuple-element.176), channel_id=1, source_target_pairs={{8,24},{9,25},{10,26},{11,27},{12,28},{13,29},{14,30},{15,31}} | collective-permute-start | bytes 2359304 | tf_op jit(solution)/shard_map/ppermute | solution.py:262
  341.2 90.3 %collective-permute-start.96 = (bf16[64,6144]{1,0:T(8,128)(2,1)}, bf16[64,6144]{1,0:T(8,128)(2,1)}, u32[]{:S(2)}, u32[]{:S(2)}) collective-permute-start(bf16[64,6144]{1,0:T(8,128)(2,1)} %get-tuple-element.176), channel_id=1, source_target_pairs={{16,24},{17,25},{18,26},{19,27},{20,28},{21,29},{22,30},{23,31}} | collective-permute-start | bytes 2359304 | tf_op jit(solution)/shard_map/ppermute | solution.py:265
  366.0 67.7 %collective-permute-start.97 = (bf16[64,6144]{1,0:T(8,128)(2,1)}, bf16[64,6144]{1,0:T(8,128)(2,1)}, u32[]{:S(2)}, u32[]{:S(2)}) collective-permute-start(bf16[64,6144]{1,0:T(8,128)(2,1)} %get-tuple-element.176), channel_id=1, source_target_pairs={{0,24},{1,25},{2,26},{3,27},{4,28},{5,29},{6,30},{7,31}} | collective-permute-start | bytes 2359304 | tf_op jit(solution)/shard_map/ppermute | solution.py:266
  396.6 20.3 %collective-permute-start.95 = (bf16[64,6144]{1,0:T(8,128)(2,1)S(1)}, bf16[64,6144]{1,0:T(8,128)(2,1)S(1)}, u32[]{:S(2)}, u32[]{:S(2)}) collective-permute-start(bf16[64,6144]{1,0:T(8,128)(2,1)S(1)} %get-tuple-element.174), channel_id=1, source_target_pairs={{16,0},{24,8},{17,1},{25,9},{18,2},{26,10},{19,3},{27,11},{20,4},{... | collective-permute-start | bytes 2359304 | tf_op jit(solution)/shard_map/ppermute | solution.py:263
  406.8 40.6 %collective-permute-start.54 = (bf16[64,3072]{1,0:T(8,128)(2,1)}, bf16[64,3072]{1,0:T(8,128)(2,1)}, u32[]{:S(2)}, u32[]{:S(2)}) collective-permute-start(bf16[64,3072]{1,0:T(8,128)(2,1)} %collective-permute-done.50), channel_id=1, source_target_pairs={{2,0},{4,6},{3,1},{5,7},{10,8},{12,14},{11,9},{13,15},{18,16},{20,... | collective-permute-start | bytes 1179656 | tf_op jit(solution)/shard_map/ppermute | solution.py:74
  416.9 45.2 %collective-permute-start.53 = (bf16[64,3072]{1,0:T(8,128)(2,1)}, bf16[64,3072]{1,0:T(8,128)(2,1)}, u32[]{:S(2)}, u32[]{:S(2)}) collective-permute-start(bf16[64,3072]{1,0:T(8,128)(2,1)} %fusion.109), channel_id=1, source_target_pairs={{0,2},{6,4},{1,3},{7,5},{8,10},{14,12},{9,11},{15,13},{16,18},{22,... | collective-permute-start | bytes 1179656 | tf_op jit(solution)/shard_map/ppermute | solution.py:74
  429.7 33.6 %collective-permute-start.52 = (bf16[64,3072]{1,0:T(8,128)(2,1)}, bf16[64,3072]{1,0:T(8,128)(2,1)}, u32[]{:S(2)}, u32[]{:S(2)}) collective-permute-start(bf16[64,3072]{1,0:T(8,128)(2,1)} %add_convert_fusion.3), channel_id=1, source_target_pairs={{2,4},{4,2},{3,5},{5,3},{10,12},{12,10},{11,13},{13,11},{18,20},{2... | collective-permute-start | bytes 1179656 | tf_op jit(solution)/shard_map/ppermute | solution.py:74
  450.8 111.9 %collective-permute-start.98 = (bf16[64,6144]{1,0:T(8,128)(2,1)S(1)}, bf16[64,6144]{1,0:T(8,128)(2,1)S(1)}, u32[]{:S(2)}, u32[]{:S(2)}) collective-permute-start(bf16[64,6144]{1,0:T(8,128)(2,1)S(1)} %get-tuple-element.173), channel_id=1, source_target_pairs={{8,24},{9,25},{10,26},{11,27},{12,28},{13,29},{14,30},{15,31}} | collective-permute-start | bytes 2359304 | tf_op jit(solution)/shard_map/ppermute | solution.py:262
  451.7 125.6 %collective-permute-start.100 = (bf16[64,6144]{1,0:T(8,128)(2,1)S(1)}, bf16[64,6144]{1,0:T(8,128)(2,1)S(1)}, u32[]{:S(2)}, u32[]{:S(2)}) collective-permute-start(bf16[64,6144]{1,0:T(8,128)(2,1)S(1)} %get-tuple-element.173), channel_id=1, source_target_pairs={{16,24},{17,25},{18,26},{19,27},{20,28},{21,29},{22,30},{23,31}} | collective-permute-start | bytes 2359304 | tf_op jit(solution)/shard_map/ppermute | solution.py:265
  452.4 164.4 %collective-permute-start.101 = (bf16[64,6144]{1,0:T(8,128)(2,1)S(1)}, bf16[64,6144]{1,0:T(8,128)(2,1)S(1)}, u32[]{:S(2)}, u32[]{:S(2)}) collective-permute-start(bf16[64,6144]{1,0:T(8,128)(2,1)S(1)} %get-tuple-element.173), channel_id=1, source_target_pairs={{0,24},{1,25},{2,26},{3,27},{4,28},{5,29},{6,30},{7,31}} | collective-permute-start | bytes 2359304 | tf_op jit(solution)/shard_map/ppermute | solution.py:266
  464.6 40.0 %collective-permute-start.106 = (bf16[64,768]{1,0:T(8,128)(2,1)S(1)}, bf16[64,768]{1,0:T(8,128)(2,1)S(1)}, u32[]{:S(2)}, u32[]{:S(2)}) collective-permute-start(bf16[64,768]{1,0:T(8,128)(2,1)S(1)} %get-tuple-element.127), channel_id=1, source_target_pairs={{8,24},{9,25},{10,26},{11,27},{12,28},{13,29},{14,30},{15,31}} | collective-permute-start | bytes 294920 | tf_op jit(solution)/shard_map/ppermute | solution.py:262
  504.6 20.3 %collective-permute-start.108 = (bf16[64,768]{1,0:T(8,128)(2,1)S(1)}, bf16[64,768]{1,0:T(8,128)(2,1)S(1)}, u32[]{:S(2)}, u32[]{:S(2)}) collective-permute-start(bf16[64,768]{1,0:T(8,128)(2,1)S(1)} %get-tuple-element.127), channel_id=1, source_target_pairs={{16,24},{17,25},{18,26},{19,27},{20,28},{21,29},{22,30},{23,31}} | collective-permute-start | bytes 294920 | tf_op jit(solution)/shard_map/ppermute | solution.py:265
  509.7 20.6 %collective-permute-start.67 = (bf16[64,3072]{1,0:T(8,128)(2,1)S(1)}, bf16[64,3072]{1,0:T(8,128)(2,1)S(1)}, u32[]{:S(2)}, u32[]{:S(2)}) collective-permute-start(bf16[64,3072]{1,0:T(8,128)(2,1)S(1)} %fusion.111), channel_id=1, source_target_pairs={{0,2},{6,4},{1,3},{7,5},{8,10},{14,12},{9,11},{15,13},{16,18},{22,... | collective-permute-start | bytes 1179656 | tf_op jit(solution)/shard_map/ppermute | solution.py:74
  528.6 34.2 %collective-permute-start.99 = (bf16[64,6144]{1,0:T(8,128)(2,1)S(1)}, bf16[64,6144]{1,0:T(8,128)(2,1)S(1)}, u32[]{:S(2)}, u32[]{:S(2)}) collective-permute-start(bf16[64,6144]{1,0:T(8,128)(2,1)S(1)} %get-tuple-element.171), channel_id=1, source_target_pairs={{16,0},{24,8},{17,1},{25,9},{18,2},{26,10},{19,3},{27,11},{20,4},{... | collective-permute-start | bytes 2359304 | tf_op jit(solution)/shard_map/ppermute | solution.py:263
  614.1 20.9 %collective-permute-start.81 = (bf16[64,6144]{1,0:T(8,128)(2,1)S(1)}, bf16[64,6144]{1,0:T(8,128)(2,1)S(1)}, u32[]{:S(2)}, u32[]{:S(2)}) collective-permute-start(bf16[64,6144]{1,0:T(8,128)(2,1)S(1)} %get-tuple-element.182), channel_id=1, source_target_pairs={{8,24},{9,25},{10,26},{11,27},{12,28},{13,29},{14,30},{15,31}} | collective-permute-start | bytes 2359304 | tf_op jit(solution)/shard_map/ppermute | solution.py:262
  614.8 20.2 %collective-permute-start.82 = (bf16[64,6144]{1,0:T(8,128)(2,1)S(1)}, bf16[64,6144]{1,0:T(8,128)(2,1)S(1)}, u32[]{:S(2)}, u32[]{:S(2)}) collective-permute-start(bf16[64,6144]{1,0:T(8,128)(2,1)S(1)} %get-tuple-element.180), channel_id=1, source_target_pairs={{16,0},{24,8},{17,1},{25,9},{18,2},{26,10},{19,3},{27,11},{20,4},{... | collective-permute-start | bytes 2359304 | tf_op jit(solution)/shard_map/ppermute | solution.py:263
  643.6 22.1 %collective-permute-start.90 = (bf16[64,6144]{1,0:T(8,128)(2,1)S(1)}, bf16[64,6144]{1,0:T(8,128)(2,1)S(1)}, u32[]{:S(2)}, u32[]{:S(2)}) collective-permute-start(bf16[64,6144]{1,0:T(8,128)(2,1)S(1)} %get-tuple-element.179), channel_id=1, source_target_pairs={{8,24},{9,25},{10,26},{11,27},{12,28},{13,29},{14,30},{15,31}} | collective-permute-start | bytes 2359304 | tf_op jit(solution)/shard_map/ppermute | solution.py:262
  644.3 21.4 %collective-permute-start.91 = (bf16[64,6144]{1,0:T(8,128)(2,1)S(1)}, bf16[64,6144]{1,0:T(8,128)(2,1)S(1)}, u32[]{:S(2)}, u32[]{:S(2)}) collective-permute-start(bf16[64,6144]{1,0:T(8,128)(2,1)S(1)} %get-tuple-element.177), channel_id=1, source_target_pairs={{16,0},{24,8},{17,1},{25,9},{18,2},{26,10},{19,3},{27,11},{20,4},{... | collective-permute-start | bytes 2359304 | tf_op jit(solution)/shard_map/ppermute | solution.py:263
  (129 other events, 2011.2 us)
